TPU v7x, 32 devices: a whole 2x2x4 slice. The times are simulated.
32 devices in a mesh: gz: 4 (over z), gy: 2 (over y), gx: 4 (over x, core).
Axes of the slice: x: 2, y: 2, z: 4, core: 2. Of those that a mesh axis runs over, the one named last changes fastest.
Arguments:
- positions: float32 [3, 12, 6, 12, 128], P(None, 'gz', 'gy', 'gx'), may hold values from 0 to 1
- velocities: float32 [3, 12, 6, 12, 128], P(None, 'gz', 'gy', 'gx'), may hold values from -6 to 6
- counts: int32 [12, 6, 12], P('gz', 'gy', 'gx'), may hold values from 64 to 128
- bonds: int32 [2, 12, 6, 12, 128], P(None, 'gz', 'gy', 'gx'), may hold values from 0 to 127
- plan_z: int32 [4], replicated, may hold values from 0 to 2
- plan_y: int32 [4, 2], replicated, may hold values from 0 to 2
- plan_x: int32 [4, 2, 4], replicated, may hold values from 0 to 2
Outputs:
- forces_first: float32 [3, 12, 6, 12, 128], P(None, 'gz', 'gy', 'gx')
- moved_positions: float32 [3, 20, 10, 20, 128], P(None, 'gz', 'gy', 'gx')
- moved_forces: float32 [3, 20, 10, 20, 128], P(None, 'gz', 'gy', 'gx')
Inputs may be any that keep to these rules, and one draw needn't show every extreme that they name: `counts`: bead b of a cell is present when b is less than the cell's count. `bonds`: both ends of a bond are bead places of the bond's own cell; a bond counts only when both ends are present. `plan_z`: entry i is the number of cells by which the boundary between brick planes i and i + 1 (the last with plane 0) moves up. `plan_y`: entry (i, j) is the number of cells by which the boundary between columns j and j + 1 of plane i (the last with column 0) moves up. `plan_x`: entry (i, j, k) is the number of cells by which the boundary between bricks k and k + 1 of column (i, j) (the last with brick 0) moves up.
All inputs are finite; a program needn't handle non-finite values.
Results may differ from a plain program's by a relative error of at most 0.0001.
Values sent between devices are 32-bit elements; how exact they have to be, the bound alone decides.
A program may use at most 64 MiB of HBM per device.

v0:
```python
import functools
import math

import jax
import jax.numpy as jnp
from jax import lax
from jax.experimental import pallas as pl
from jax.experimental.pallas import tpu as pltpu
from jax.sharding import PartitionSpec as P

STRENGTH = 0.3
SPREAD = 0.6
BOND_STIFF = 1.0
STEP_DT = 0.2
FAR_AWAY = 1000.0
UNIT = math.sqrt(1.0 / (SPREAD * math.log(2.0)))
ROWS = 16


def from_behind(block, axis, distance):
    devices = range(lax.axis_size(axis))
    route = [((i - distance) % len(devices), i) for i in devices]
    return lax.ppermute(block, axis, route)


def split_three(values):
    high = values.astype(jnp.bfloat16)
    rest = values - high.astype(jnp.float32)
    middle = rest.astype(jnp.bfloat16)
    low = (rest - middle.astype(jnp.float32)).astype(jnp.bfloat16)
    return high, middle, low


def bond_kernel(side, counts_ref, bonds_ref, lap_ref):
    beads = lap_ref.shape[-1]
    bond_count = bonds_ref.shape[-1]

    def one_row(row, carry):
        z, y = row // side, lax.rem(row, side)
        bead = lax.broadcasted_iota(jnp.int32, (beads, bond_count), 0)
        for x in range(side):
            count = counts_ref[z, y, x]
            head = bonds_ref[0, z, y, x : x + 1, :]
            tail = bonds_ref[1, z, y, x : x + 1, :]
            alive = ((head < count) & (tail < count)).astype(jnp.float32)
            ends = jnp.where(bead == head, alive, 0.0) - jnp.where(bead == tail, alive, 0.0)
            ends = ends.astype(jnp.bfloat16)
            lap_ref[row, x] = lax.dot_general(
                ends, ends, (((1,), (1,)), ((), ())), preferred_element_type=jnp.float32
            ).astype(jnp.bfloat16)
        return carry

    lax.fori_loop(0, side * side, one_row, 0)


def force_kernel(side, counts_ref, ext_ref, lap_ref, out_ref, grid_ref, own_ref, sum_ref):
    beads = ext_ref.shape[-1]
    wide = side + 2
    padded = grid_ref.shape[3]

    shape = (wide, wide, wide, beads)
    for k in range(3):
        shift = lax.broadcasted_iota(jnp.int32, shape, k).astype(jnp.float32)
        grid_ref[k, :, :, 0:wide, :] = (ext_ref[k] + shift) * UNIT

    def one_row(row, carry):
        z, y = row // side, lax.rem(row, side)
        tile = jnp.concatenate(
            [grid_ref[k, z + 1, y + 1] for k in range(3)], axis=0
        )
        columns = tile.T
        for k in range(3):
            for x in range(side):
                place = k * padded + x + 1
                own_ref[k * side + x] = jnp.broadcast_to(
                    columns[:, place : place + 1], (beads, beads)
                )
        for x in range(side):
            count = counts_ref[z, y, x]

            def one_block(i, inner):
                rows = pl.ds(pl.multiple_of(i * ROWS, ROWS), ROWS)
                own = [own_ref[k * side + x, rows, :] for k in range(3)]
                total = [jnp.zeros((ROWS, beads), jnp.float32) for _ in range(3)]
                for dz in range(3):
                    for dy in range(3):
                        for dx in range(3):
                            apart = [
                                own[k]
                                - grid_ref[k, z + dz, y + dy, x + dx : x + dx + 1, :]
                                for k in range(3)
                            ]
                            distance = (
                                apart[0] * apart[0] + apart[1] * apart[1] + apart[2] * apart[2]
                            )
                            weight = jnp.exp2(-distance)
                            total = [total[k] + weight * apart[k] for k in range(3)]
                for k in range(3):
                    sum_ref[k * side + x, rows, :] = total[k]
                return inner

            lax.fori_loop(0, (count + (ROWS - 1)) // ROWS, one_block, 0)
        lane = lax.broadcasted_iota(jnp.int32, (1, beads), 1)
        for x in range(side):
            count = counts_ref[z, y, x]
            high, middle, low = split_three(
                jnp.concatenate(
                    [grid_ref[k, z + 1, y + 1, x + 1 : x + 2, :] for k in range(3)]
                    + [jnp.zeros((5, beads), jnp.float32)],
                    axis=0,
                )
            )
            lap = lap_ref[row, x]
            bond = (
                jnp.dot(low, lap, preferred_element_type=jnp.float32)
                + jnp.dot(middle, lap, preferred_element_type=jnp.float32)
                + jnp.dot(high, lap, preferred_element_type=jnp.float32)
            )
            for k in range(3):
                pair = jnp.sum(sum_ref[k * side + x].T, axis=0, keepdims=True)
                force = (STRENGTH / UNIT) * pair - (BOND_STIFF / UNIT) * bond[k : k + 1]
                out_ref[k, z, y, x : x + 1, :] = jnp.where(lane < count, force, 0.0)
        return carry

    lax.fori_loop(0, side * side, one_row, 0)


def bond_matrices(counts, bonds, beads):
    side = counts.shape[0]
    return pl.pallas_call(
        functools.partial(bond_kernel, side),
        out_shape=jax.ShapeDtypeStruct((side * side, side, beads, beads), jnp.bfloat16),
        in_specs=[
            pl.BlockSpec(memory_space=pltpu.SMEM),
            pl.BlockSpec(memory_space=pltpu.VMEM),
        ],
        out_specs=pl.BlockSpec(memory_space=pltpu.VMEM),
        compiler_params=pltpu.CompilerParams(vmem_limit_bytes=40 * 1024 * 1024),
        name="bond_matrices",
    )(counts, bonds)


def local_forces(extended, counts, laps):
    side = counts.shape[0]
    beads = extended.shape[-1]
    wide = side + 2
    padded = -(-wide // 8) * 8
    return pl.pallas_call(
        functools.partial(force_kernel, side),
        out_shape=jax.ShapeDtypeStruct((3, side, side, side, beads), jnp.float32),
        in_specs=[
            pl.BlockSpec(memory_space=pltpu.SMEM),
            pl.BlockSpec(memory_space=pltpu.VMEM),
            pl.BlockSpec(memory_space=pltpu.VMEM),
        ],
        out_specs=pl.BlockSpec(memory_space=pltpu.VMEM),
        scratch_shapes=[
            pltpu.VMEM((3, wide, wide, padded, beads), jnp.float32),
            pltpu.VMEM((3 * side, beads, beads), jnp.float32),
            pltpu.VMEM((3 * side, beads, beads), jnp.float32),
        ],
        compiler_params=pltpu.CompilerParams(vmem_limit_bytes=40 * 1024 * 1024),
        name="cell_forces",
    )(counts, extended, laps)


def halo_extend(parked):
    grown = parked
    for dim, axis in ((1, "gz"), (2, "gy"), (3, "gx")):
        size = grown.shape[dim]
        below = from_behind(lax.slice_in_dim(grown, size - 1, size, axis=dim), axis, 1)
        above = from_behind(lax.slice_in_dim(grown, 0, 1, axis=dim), axis, -1)
        grown = jnp.concatenate([below, grown, above], axis=dim)
    return grown


def pick_entry(plan_table, position):
    matched = jnp.arange(plan_table.shape[0], dtype=jnp.int32) == position
    return jnp.sum(
        jnp.where(matched.reshape((-1,) + (1,) * (plan_table.ndim - 1)), plan_table, 0), axis=0
    )


def hand_over(blocks, arrival, which_axis, lowered, raised, side_cells):
    joined = jnp.concatenate([blocks, arrival, jnp.zeros_like(arrival)], axis=which_axis)
    kept_part = lax.dynamic_slice_in_dim(joined, lowered, side_cells + 2, axis=which_axis)
    filled = side_cells + raised - lowered
    usable = (jnp.arange(side_cells + 2, dtype=jnp.int32) < filled).astype(jnp.float32)
    shape_list = [1] * blocks.ndim
    shape_list[which_axis] = side_cells + 2
    return kept_part * usable.reshape(shape_list)


def on_device(positions, velocities, counts, bonds, plan_z, plan_y, plan_x):
    side_cells = positions.shape[1]
    bead_count = positions.shape[-1]
    living = (jnp.arange(bead_count, dtype=jnp.int32) < counts[..., None]).astype(jnp.float32)
    laps = bond_matrices(counts, bonds, bead_count)
    parked = jnp.where(living[None] > 0, positions, FAR_AWAY)
    forces_first = local_forces(halo_extend(parked), counts, laps)
    stepped = positions + STEP_DT * velocities + 0.5 * STEP_DT * STEP_DT * forces_first
    parked = jnp.where(living[None] > 0, stepped, FAR_AWAY)
    forces_next = local_forces(halo_extend(parked), counts, laps)
    carried = jnp.concatenate([stepped * living[None], forces_next], axis=0)
    plane_index = lax.axis_index("gz")
    column_index = lax.axis_index("gy")
    brick_index = lax.axis_index("gx")
    plane_total = lax.axis_size("gz")
    column_total = lax.axis_size("gy")
    brick_total = lax.axis_size("gx")
    lowered_z = pick_entry(plan_z, (plane_index + plane_total - 1) % plane_total)
    raised_z = pick_entry(plan_z, plane_index)
    plane_row = pick_entry(plan_y, plane_index)
    lowered_y = pick_entry(plane_row, (column_index + column_total - 1) % column_total)
    raised_y = pick_entry(plane_row, column_index)
    column_row = pick_entry(pick_entry(plan_x, plane_index), column_index)
    lowered_x = pick_entry(column_row, (brick_index + brick_total - 1) % brick_total)
    raised_x = pick_entry(column_row, brick_index)
    arrival = from_behind(lax.slice_in_dim(carried, 0, 2, axis=1), "gz", -1)
    carried = hand_over(carried, arrival, 1, lowered_z, raised_z, side_cells)
    arrival = from_behind(lax.slice_in_dim(carried, 0, 2, axis=2), "gy", -1)
    carried = hand_over(carried, arrival, 2, lowered_y, raised_y, side_cells)
    arrival = from_behind(lax.slice_in_dim(carried, 0, 2, axis=3), "gx", -1)
    carried = hand_over(carried, arrival, 3, lowered_x, raised_x, side_cells)
    return (forces_first, carried[:3], carried[3:])


def solution(mesh):
    return jax.shard_map(
        on_device,
        mesh=mesh,
        in_specs=(
            P(None, "gz", "gy", "gx", None),
            P(None, "gz", "gy", "gx", None),
            P("gz", "gy", "gx"),
            P(None, "gz", "gy", "gx", None),
            P(),
            P(),
            P(),
        ),
        out_specs=(
            P(None, "gz", "gy", "gx", None),
            P(None, "gz", "gy", "gx", None),
            P(None, "gz", "gy", "gx", None),
        ),
        check_vma=False,
    )
```

profile of v0, /device:TPU:1, one launch (start us, length us, event | category | flops | bytes accessed | tf_op | source)
XLA Modules:
  0.0 117.7 jit_solution(15973864508251092267)
XLA Ops:
  0.6 0.8 fusion.9
  1.4 0.8 broadcast_select_fusion.1
  2.3 2.2 %collective-permute-start = (f32[3,1,3,3,128]{4,3,2,1,0:T(4,128)S(1)}, f32[3,1,3,3,128]{4,3,2,1,0:T(4,128)S(1)}, u32[]{:S(2)}, u32[]{:S(2)}) collective-permute-start(f32[3,1,3,3,128]{4,3,2,1,0:T(4,128)S(1)} %get-tuple-element.29), channel_id=1, source_target_pairs={{24,0},{0,8},{8,16},{16,24},{25,1},{1,9},{9,17},{17,25},{26,2},{2,... | collective-permute-start | bytes 41480 | tf_op jit(solution)/shard_map/ppermute | solution.py:23
  4.4 2.1 %collective-permute-start.1 = (f32[3,1,3,3,128]{4,3,2,1,0:T(4,128)S(1)}, f32[3,1,3,3,128]{4,3,2,1,0:T(4,128)S(1)}, u32[]{:S(2)}, u32[]{:S(2)}) collective-permute-start(f32[3,1,3,3,128]{4,3,2,1,0:T(4,128)S(1)} %get-tuple-element.30), channel_id=1, source_target_pairs={{8,0},{16,8},{24,16},{0,24},{9,1},{17,9},{25,17},{1,25},{10,2},{18... | collective-permute-start | bytes 41480 | tf_op jit(solution)/shard_map/ppermute | solution.py:23
  6.5 0.7 copy-done.4
  7.2 0.1 select_reduce_fusion
  7.3 0.3 collective-permute-done
  7.6 1.3 %collective-permute-start.2 = (f32[3,5,1,3,128]{4,3,2,1,0:T(4,128)S(1)}, f32[3,5,1,3,128]{4,3,2,1,0:T(4,128)S(1)}, u32[]{:S(2)}, u32[]{:S(2)}) collective-permute-start(f32[3,5,1,3,128]{4,3,2,1,0:T(4,128)S(1)} %get-tuple-element.25), channel_id=1, source_target_pairs={{4,0},{0,4},{5,1},{1,5},{6,2},{2,6},{7,3},{3,7},{12,8},{8,12},{13,... | collective-permute-start | bytes 69128 | tf_op jit(solution)/shard_map/ppermute | solution.py:23
  8.9 0.2 collective-permute-start.3
  9.2 0.1 select_reduce_fusion.1
  9.3 1.2 %collective-permute-done.2 = f32[3,5,1,3,128]{4,3,2,1,0:T(4,128)S(1)} collective-permute-done((f32[3,5,1,3,128]{4,3,2,1,0:T(4,128)S(1)}, f32[3,5,1,3,128]{4,3,2,1,0:T(4,128)S(1)}, u32[]{:S(2)}, u32[]{:S(2)}) %collective-permute-start.2) | collective-permute-done | bytes 23072 | tf_op jit(solution)/shard_map/ppermute | solution.py:23
  10.4 1.2 %collective-permute-done.3 = f32[3,5,1,3,128]{4,3,2,1,0:T(4,128)S(1)} collective-permute-done((f32[3,5,1,3,128]{4,3,2,1,0:T(4,128)S(1)}, f32[3,5,1,3,128]{4,3,2,1,0:T(4,128)S(1)}, u32[]{:S(2)}, u32[]{:S(2)}) %collective-permute-start.3) | collective-permute-done | bytes 23072 | tf_op jit(solution)/shard_map/ppermute | solution.py:23
  11.7 0.1 pad_maximum_fusion.12
  11.8 0.0 copy-start.6
  11.8 4.3 %collective-permute-start.4 = (f32[3,5,5,1,128]{4,3,2,1,0:T(1,128)S(1)}, f32[3,5,5,1,128]{4,3,2,1,0:T(1,128)S(1)}, u32[]{:S(2)}, u32[]{:S(2)}) collective-permute-start(f32[3,5,5,1,128]{4,3,2,1,0:T(1,128)S(1)} %get-tuple-element.21), channel_id=1, source_target_pairs={{3,0},{0,1},{1,2},{2,3},{7,4},{4,5},{5,6},{6,7},{11,8},{8,9},{9,10... | collective-permute-start | bytes 115208 | tf_op jit(solution)/shard_map/ppermute | solution.py:23
  16.1 0.7 fusion.13
  16.9 0.7 copy-done
  17.5 2.6 %bond_matrices.1.lap_ref = bf16[9,3,128,128]{3,2,1,0:T(8,128)(2,1)S(1)} custom-call(s32[3,3,3]{2,1,0:T(4,128)S(1)} %copy-done, s32[2,3,3,3,128]{4,3,2,1,0:T(4,128)S(1)} %copy.13.bonds_ref), custom_call_target="tpu_custom_call" | custom-call | tf_op jit(solution)/shard_map/bond_matrices/pallas_call | solution.py:130
  20.2 0.1 pad_maximum_fusion.ext_ref
  20.3 0.0 copy-start.1
  20.3 31.0 %cell_forces.2 = f32[3,3,3,3,128]{4,3,2,1,0:T(4,128)} custom-call(s32[3,3,3]{2,1,0:T(4,128)S(1)} %copy-done, f32[3,5,5,5,128]{4,3,2,1,0:T(8,128)S(1)} %pad_maximum_fusion.ext_ref, bf16[9,3,128,128]{3,2,1,0:T(8,128)(2,1)S(1)} %bond_matrices.1.lap_ref), custom_call_target="tpu_custom_call" | custom-call | tf_op jit(solution)/shard_map/cell_forces/pallas_call | solution.py:148
  51.3 0.9 broadcast_select_fusion
  52.1 0.0 copy-start.5
  52.2 1.3 %collective-permute-start.6 = (f32[3,1,3,3,128]{4,3,2,1,0:T(4,128)S(1)}, f32[3,1,3,3,128]{4,3,2,1,0:T(4,128)S(1)}, u32[]{:S(2)}, u32[]{:S(2)}) collective-permute-start(f32[3,1,3,3,128]{4,3,2,1,0:T(4,128)S(1)} %get-tuple-element.27), channel_id=1, source_target_pairs={{24,0},{0,8},{8,16},{16,24},{25,1},{1,9},{9,17},{17,25},{26,2},{2,... | collective-permute-start | bytes 41480 | tf_op jit(solution)/shard_map/ppermute | solution.py:23
  53.4 2.1 %collective-permute-start.7 = (f32[3,1,3,3,128]{4,3,2,1,0:T(4,128)S(1)}, f32[3,1,3,3,128]{4,3,2,1,0:T(4,128)S(1)}, u32[]{:S(2)}, u32[]{:S(2)}) collective-permute-start(f32[3,1,3,3,128]{4,3,2,1,0:T(4,128)S(1)} %get-tuple-element.28), channel_id=1, source_target_pairs={{8,0},{16,8},{24,16},{0,24},{9,1},{17,9},{25,17},{1,25},{10,2},{18... | collective-permute-start | bytes 41480 | tf_op jit(solution)/shard_map/ppermute | solution.py:23
  55.5 0.1 select_reduce_fusion.2
  55.6 1.0 collective-permute-done.6
  56.6 0.7 collective-permute-start.8
  57.3 0.9 collective-permute-start.9
  58.2 0.7 select_reduce_fusion.3
  64.4 0.1 pad_maximum_fusion.7
  64.5 3.6 %collective-permute-start.10 = (f32[3,5,5,1,128]{4,3,2,1,0:T(1,128)S(1)}, f32[3,5,5,1,128]{4,3,2,1,0:T(1,128)S(1)}, u32[]{:S(2)}, u32[]{:S(2)}) collective-permute-start(f32[3,5,5,1,128]{4,3,2,1,0:T(1,128)S(1)} %get-tuple-element.19), channel_id=1, source_target_pairs={{3,0},{0,1},{1,2},{2,3},{7,4},{4,5},{5,6},{6,7},{11,8},{8,9},{9,10... | collective-permute-start | bytes 115208 | tf_op jit(solution)/shard_map/ppermute | solution.py:23
  68.1 0.1 pad_dynamic-slice_fusion.5
  69.5 2.0 %collective-permute-done.11 = f32[3,5,5,1,128]{4,3,2,1,0:T(1,128)S(1)} collective-permute-done((f32[3,5,5,1,128]{4,3,2,1,0:T(1,128)S(1)}, f32[3,5,5,1,128]{4,3,2,1,0:T(1,128)S(1)}, u32[]{:S(2)}, u32[]{:S(2)}) %collective-permute-start.11) | collective-permute-done | bytes 38432 | tf_op jit(solution)/shard_map/ppermute | solution.py:23
  71.5 0.1 pad_maximum_fusion.1.ext_ref
  71.6 30.3 %cell_forces.3 = f32[3,3,3,3,128]{4,3,2,1,0:T(4,128)S(1)} custom-call(s32[3,3,3]{2,1,0:T(4,128)S(1)} %copy-done, f32[3,5,5,5,128]{4,3,2,1,0:T(8,128)S(1)} %pad_maximum_fusion.1.ext_ref, bf16[9,3,128,128]{3,2,1,0:T(8,128)(2,1)S(1)} %bond_matrices.1.lap_ref), custom_call_target="tpu_custom_call" | custom-call | tf_op jit(solution)/shard_map/cell_forces/pallas_call | solution.py:148
  102.0 2.3 %collective-permute-start.12 = (f32[6,2,3,3,128]{4,3,2,1,0:T(4,128)S(1)}, f32[6,2,3,3,128]{4,3,2,1,0:T(4,128)S(1)}, u32[]{:S(2)}, u32[]{:S(2)}) collective-permute-start(f32[6,2,3,3,128]{4,3,2,1,0:T(4,128)S(1)} %pad_maximum_fusion.2), channel_id=1, source_target_pairs={{8,0},{16,8},{24,16},{0,24},{9,1},{17,9},{25,17},{1,25},{10,2},{18... | collective-permute-start | bytes 165896 | tf_op jit(solution)/shard_map/ppermute | solution.py:23
  105.5 0.1 collective-permute-done.12
  105.6 0.1 fusion.8
  105.8 1.0 collective-permute-start.13
  106.7 4.0 %collective-permute-done.13 = f32[6,5,2,3,128]{4,3,2,1,0:T(4,128)S(1)} collective-permute-done((f32[6,5,2,3,128]{4,3,2,1,0:T(4,128)S(1)}, f32[6,5,2,3,128]{4,3,2,1,0:T(4,128)S(1)}, u32[]{:S(2)}, u32[]{:S(2)}) %collective-permute-start.13) | collective-permute-done | bytes 92192 | tf_op jit(solution)/shard_map/ppermute | solution.py:23
  110.8 0.1 fusion.4
  110.9 0.1 slice.73
  111.0 0.4 collective-permute-start.14
  112.7 3.1 %collective-permute-done.14 = f32[6,5,5,2,128]{4,3,2,1,0:T(2,128)S(1)} collective-permute-done((f32[6,5,5,2,128]{4,3,2,1,0:T(2,128)S(1)}, f32[6,5,5,2,128]{4,3,2,1,0:T(2,128)S(1)}, u32[]{:S(2)}, u32[]{:S(2)}) %collective-permute-start.14) | collective-permute-done | bytes 153632 | tf_op jit(solution)/shard_map/ppermute | solution.py:23
  115.9 0.3 fusion.1
  116.2 0.8 copy.14
  117.0 0.8 copy.15
  (32 shorter events, 0.2 us)
Async XLA Ops:
  2.3 5.4 %collective-permute-start = (f32[3,1,3,3,128]{4,3,2,1,0:T(4,128)S(1)}, f32[3,1,3,3,128]{4,3,2,1,0:T(4,128)S(1)}, u32[]{:S(2)}, u32[]{:S(2)}) collective-permute-start(f32[3,1,3,3,128]{4,3,2,1,0:T(4,128)S(1)} %get-tuple-element.29), channel_id=1, source_target_pairs={{24,0},{0,8},{8,16},{16,24},{25,1},{1,9},{9,17},{17,25},{26,2},{2,... | collective-permute-start | bytes 41480 | tf_op jit(solution)/shard_map/ppermute | solution.py:23
  4.4 3.2 %collective-permute-start.1 = (f32[3,1,3,3,128]{4,3,2,1,0:T(4,128)S(1)}, f32[3,1,3,3,128]{4,3,2,1,0:T(4,128)S(1)}, u32[]{:S(2)}, u32[]{:S(2)}) collective-permute-start(f32[3,1,3,3,128]{4,3,2,1,0:T(4,128)S(1)} %get-tuple-element.30), channel_id=1, source_target_pairs={{8,0},{16,8},{24,16},{0,24},{9,1},{17,9},{25,17},{1,25},{10,2},{18... | collective-permute-start | bytes 41480 | tf_op jit(solution)/shard_map/ppermute | solution.py:23
  6.5 0.7 copy-start.4
  7.6 2.8 %collective-permute-start.2 = (f32[3,5,1,3,128]{4,3,2,1,0:T(4,128)S(1)}, f32[3,5,1,3,128]{4,3,2,1,0:T(4,128)S(1)}, u32[]{:S(2)}, u32[]{:S(2)}) collective-permute-start(f32[3,5,1,3,128]{4,3,2,1,0:T(4,128)S(1)} %get-tuple-element.25), channel_id=1, source_target_pairs={{4,0},{0,4},{5,1},{1,5},{6,2},{2,6},{7,3},{3,7},{12,8},{8,12},{13,... | collective-permute-start | bytes 69128 | tf_op jit(solution)/shard_map/ppermute | solution.py:23
  8.9 2.7 %collective-permute-start.3 = (f32[3,5,1,3,128]{4,3,2,1,0:T(4,128)S(1)}, f32[3,5,1,3,128]{4,3,2,1,0:T(4,128)S(1)}, u32[]{:S(2)}, u32[]{:S(2)}) collective-permute-start(f32[3,5,1,3,128]{4,3,2,1,0:T(4,128)S(1)} %get-tuple-element.26), channel_id=1, source_target_pairs={{4,0},{0,4},{5,1},{1,5},{6,2},{2,6},{7,3},{3,7},{12,8},{8,12},{13,... | collective-permute-start | bytes 69128 | tf_op jit(solution)/shard_map/ppermute | solution.py:23
  11.7 5.2 %copy-start.3 = (s32[2,3,3,3,128]{4,0,3,2,1:T(2,128)S(1)}, s32[2,3,3,3,128]{4,0,3,2,1:T(2,128)}, u32[]{:S(2)}) copy-start(s32[2,3,3,3,128]{4,0,3,2,1:T(2,128)} %param.10) | copy-start | bytes 82948
  11.8 4.4 %copy-start.6 = (s32[4]{0:T(128)S(1)}, s32[4]{0:T(128)}, u32[]{:S(2)}) copy-start(s32[4]{0:T(128)} %param.11) | copy-start | bytes 52
  11.8 8.4 %collective-permute-start.4 = (f32[3,5,5,1,128]{4,3,2,1,0:T(1,128)S(1)}, f32[3,5,5,1,128]{4,3,2,1,0:T(1,128)S(1)}, u32[]{:S(2)}, u32[]{:S(2)}) collective-permute-start(f32[3,5,5,1,128]{4,3,2,1,0:T(1,128)S(1)} %get-tuple-element.21), channel_id=1, source_target_pairs={{3,0},{0,1},{1,2},{2,3},{7,4},{4,5},{5,6},{6,7},{11,8},{8,9},{9,10... | collective-permute-start | bytes 115208 | tf_op jit(solution)/shard_map/ppermute | solution.py:23
  16.1 4.1 %collective-permute-start.5 = (f32[3,5,5,1,128]{4,3,2,1,0:T(1,128)S(1)}, f32[3,5,5,1,128]{4,3,2,1,0:T(1,128)S(1)}, u32[]{:S(2)}, u32[]{:S(2)}) collective-permute-start(f32[3,5,5,1,128]{4,3,2,1,0:T(1,128)S(1)} %get-tuple-element.22), channel_id=1, source_target_pairs={{1,0},{2,1},{3,2},{0,3},{5,4},{6,5},{7,6},{4,7},{9,8},{10,9},{11,1... | collective-permute-start | bytes 115208 | tf_op jit(solution)/shard_map/ppermute | solution.py:23
  16.9 0.7 copy-start
  20.3 31.0 %copy-start.1 = (f32[3,3,3,3,128]{4,3,2,1,0:T(4,128)S(1)}, f32[3,3,3,3,128]{4,3,2,1,0:T(4,128)}, u32[]{:S(2)}) copy-start(f32[3,3,3,3,128]{4,3,2,1,0:T(4,128)} %param.7) | copy-start | bytes 124420
  20.3 31.0 %copy-start.2 = (f32[3,3,3,3,128]{4,3,2,1,0:T(4,128)S(1)}, f32[3,3,3,3,128]{4,3,2,1,0:T(4,128)}, u32[]{:S(2)}) copy-start(f32[3,3,3,3,128]{4,3,2,1,0:T(4,128)} %param.8) | copy-start | bytes 124420
  52.1 3.3 %copy-start.5 = (s32[4,2]{0,1:T(2,128)S(1)}, s32[4,2]{0,1:T(2,128)}, u32[]{:S(2)}) copy-start(s32[4,2]{0,1:T(2,128)} %param.12) | copy-start | bytes 100
  52.2 4.5 %collective-permute-start.6 = (f32[3,1,3,3,128]{4,3,2,1,0:T(4,128)S(1)}, f32[3,1,3,3,128]{4,3,2,1,0:T(4,128)S(1)}, u32[]{:S(2)}, u32[]{:S(2)}) collective-permute-start(f32[3,1,3,3,128]{4,3,2,1,0:T(4,128)S(1)} %get-tuple-element.27), channel_id=1, source_target_pairs={{24,0},{0,8},{8,16},{16,24},{25,1},{1,9},{9,17},{17,25},{26,2},{2,... | collective-permute-start | bytes 41480 | tf_op jit(solution)/shard_map/ppermute | solution.py:23
  53.4 3.2 %collective-permute-start.7 = (f32[3,1,3,3,128]{4,3,2,1,0:T(4,128)S(1)}, f32[3,1,3,3,128]{4,3,2,1,0:T(4,128)S(1)}, u32[]{:S(2)}, u32[]{:S(2)}) collective-permute-start(f32[3,1,3,3,128]{4,3,2,1,0:T(4,128)S(1)} %get-tuple-element.28), channel_id=1, source_target_pairs={{8,0},{16,8},{24,16},{0,24},{9,1},{17,9},{25,17},{1,25},{10,2},{18... | collective-permute-start | bytes 41480 | tf_op jit(solution)/shard_map/ppermute | solution.py:23
  56.6 7.7 %collective-permute-start.8 = (f32[3,5,1,3,128]{4,3,2,1,0:T(4,128)S(1)}, f32[3,5,1,3,128]{4,3,2,1,0:T(4,128)S(1)}, u32[]{:S(2)}, u32[]{:S(2)}) collective-permute-start(f32[3,5,1,3,128]{4,3,2,1,0:T(4,128)S(1)} %get-tuple-element.23), channel_id=1, source_target_pairs={{4,0},{0,4},{5,1},{1,5},{6,2},{2,6},{7,3},{3,7},{12,8},{8,12},{13,... | collective-permute-start | bytes 69128 | tf_op jit(solution)/shard_map/ppermute | solution.py:23
  57.3 7.1 %collective-permute-start.9 = (f32[3,5,1,3,128]{4,3,2,1,0:T(4,128)S(1)}, f32[3,5,1,3,128]{4,3,2,1,0:T(4,128)S(1)}, u32[]{:S(2)}, u32[]{:S(2)}) collective-permute-start(f32[3,5,1,3,128]{4,3,2,1,0:T(4,128)S(1)} %get-tuple-element.24), channel_id=1, source_target_pairs={{4,0},{0,4},{5,1},{1,5},{6,2},{2,6},{7,3},{3,7},{12,8},{8,12},{13,... | collective-permute-start | bytes 69128 | tf_op jit(solution)/shard_map/ppermute | solution.py:23
  64.5 5.0 %collective-permute-start.10 = (f32[3,5,5,1,128]{4,3,2,1,0:T(1,128)S(1)}, f32[3,5,5,1,128]{4,3,2,1,0:T(1,128)S(1)}, u32[]{:S(2)}, u32[]{:S(2)}) collective-permute-start(f32[3,5,5,1,128]{4,3,2,1,0:T(1,128)S(1)} %get-tuple-element.19), channel_id=1, source_target_pairs={{3,0},{0,1},{1,2},{2,3},{7,4},{4,5},{5,6},{6,7},{11,8},{8,9},{9,10... | collective-permute-start | bytes 115208 | tf_op jit(solution)/shard_map/ppermute | solution.py:23
  68.1 3.4 %collective-permute-start.11 = (f32[3,5,5,1,128]{4,3,2,1,0:T(1,128)S(1)}, f32[3,5,5,1,128]{4,3,2,1,0:T(1,128)S(1)}, u32[]{:S(2)}, u32[]{:S(2)}) collective-permute-start(f32[3,5,5,1,128]{4,3,2,1,0:T(1,128)S(1)} %get-tuple-element.20), channel_id=1, source_target_pairs={{1,0},{2,1},{3,2},{0,3},{5,4},{6,5},{7,6},{4,7},{9,8},{10,9},{11,1... | collective-permute-start | bytes 115208 | tf_op jit(solution)/shard_map/ppermute | solution.py:23
  102.0 3.7 %collective-permute-start.12 = (f32[6,2,3,3,128]{4,3,2,1,0:T(4,128)S(1)}, f32[6,2,3,3,128]{4,3,2,1,0:T(4,128)S(1)}, u32[]{:S(2)}, u32[]{:S(2)}) collective-permute-start(f32[6,2,3,3,128]{4,3,2,1,0:T(4,128)S(1)} %pad_maximum_fusion.2), channel_id=1, source_target_pairs={{8,0},{16,8},{24,16},{0,24},{9,1},{17,9},{25,17},{1,25},{10,2},{18... | collective-permute-start | bytes 165896 | tf_op jit(solution)/shard_map/ppermute | solution.py:23
  105.8 5.0 %collective-permute-start.13 = (f32[6,5,2,3,128]{4,3,2,1,0:T(4,128)S(1)}, f32[6,5,2,3,128]{4,3,2,1,0:T(4,128)S(1)}, u32[]{:S(2)}, u32[]{:S(2)}) collective-permute-start(f32[6,5,2,3,128]{4,3,2,1,0:T(4,128)S(1)} %slice.72), channel_id=1, source_target_pairs={{4,0},{0,4},{5,1},{1,5},{6,2},{2,6},{7,3},{3,7},{12,8},{8,12},{13,... | collective-permute-start | bytes 276488 | tf_op jit(solution)/shard_map/ppermute | solution.py:23
  111.0 4.9 %collective-permute-start.14 = (f32[6,5,5,2,128]{4,3,2,1,0:T(2,128)S(1)}, f32[6,5,5,2,128]{4,3,2,1,0:T(2,128)S(1)}, u32[]{:S(2)}, u32[]{:S(2)}) collective-permute-start(f32[6,5,5,2,128]{4,3,2,1,0:T(2,128)S(1)} %slice.73), channel_id=1, source_target_pairs={{1,0},{2,1},{3,2},{0,3},{5,4},{6,5},{7,6},{4,7},{9,8},{10,9},{11,1... | collective-permute-start | bytes 460808 | tf_op jit(solution)/shard_map/ppermute | solution.py:23
where the time goes:
time: 119 us; the launch traced here: 118 us
  Pallas kernels  63.9 us (54%)
  starting transfers between devices  22.3 us (19%)
  waiting for transfers between devices  13.1 us (11%)
  between operations  10.2 us (9%)
  other arithmetic  5.09 us (4%)
  local copies, waits for them, and re-layouts  3.15 us (3%)
    pallas_call x2, Pallas kernels, local_forces(): pl.pallas_call(functools.partial(force_kernel, side), out_shape=jax.Shape...  61.3 us
    ppermute x15, starting transfers between devices, from_behind(): return lax.ppermute(block, axis, route)  22.3 us
    ppermute x15, waiting for transfers between devices, from_behind(): return lax.ppermute(block, axis, route)  13.1 us
    unnamed x17, local copies, waits for them, and re-layouts  2.92 us
    pallas_call x1, Pallas kernels, bond_matrices(): pl.pallas_call(functools.partial(bond_kernel, side), out_shape=jax.ShapeD...  2.6 us
  transfers between devices with their start and end apart: 15, of which 8 were waited for; matrix products, arithmetic and copies ran while one was open for 2% of the time, Pallas kernels for 2%

commit v1 on v0

--- a/solution.py
+++ b/solution.py
@@ -14,7 +14,7 @@
 STEP_DT = 0.2
 FAR_AWAY = 1000.0
 UNIT = math.sqrt(1.0 / (SPREAD * math.log(2.0)))
-ROWS = 16
+ROWS = 32
 
 
 def from_behind(block, axis, distance):
@@ -24,11 +24,10 @@
 
 
 def split_three(values):
-    high = values.astype(jnp.bfloat16)
-    rest = values - high.astype(jnp.float32)
-    middle = rest.astype(jnp.bfloat16)
-    low = (rest - middle.astype(jnp.float32)).astype(jnp.bfloat16)
-    return high, middle, low
+    high = values.astype(jnp.bfloat16).astype(jnp.float32)
+    rest = values - high
+    middle = rest.astype(jnp.bfloat16).astype(jnp.float32)
+    return [high, middle, rest - middle]
 
 
 def bond_kernel(side, counts_ref, bonds_ref, lap_ref):
@@ -103,19 +102,18 @@
         lane = lax.broadcasted_iota(jnp.int32, (1, beads), 1)
         for x in range(side):
             count = counts_ref[z, y, x]
-            high, middle, low = split_three(
+            parts = split_three(
                 jnp.concatenate(
                     [grid_ref[k, z + 1, y + 1, x + 1 : x + 2, :] for k in range(3)]
                     + [jnp.zeros((5, beads), jnp.float32)],
                     axis=0,
                 )
             )
-            lap = lap_ref[row, x]
-            bond = (
-                jnp.dot(low, lap, preferred_element_type=jnp.float32)
-                + jnp.dot(middle, lap, preferred_element_type=jnp.float32)
-                + jnp.dot(high, lap, preferred_element_type=jnp.float32)
+            stacked = jnp.concatenate(parts + [jnp.zeros((8, beads), jnp.float32)], axis=0)
+            product = jnp.dot(
+                stacked.astype(jnp.bfloat16), lap_ref[row, x], preferred_element_type=jnp.float32
             )
+            bond = product[16:24] + product[8:16] + product[0:8]
             for k in range(3):
                 pair = jnp.sum(sum_ref[k * side + x].T, axis=0, keepdims=True)
                 force = (STRENGTH / UNIT) * pair - (BOND_STIFF / UNIT) * bond[k : k + 1]
@@ -136,6 +134,9 @@
         ],
         out_specs=pl.BlockSpec(memory_space=pltpu.VMEM),
         compiler_params=pltpu.CompilerParams(vmem_limit_bytes=40 * 1024 * 1024),
+        cost_estimate=pl.CostEstimate(
+            flops=2 * side**3 * beads**3, bytes_accessed=2 * side**3 * beads**2, transcendentals=0
+        ),
         name="bond_matrices",
     )(counts, bonds)
 

time: 119 us -> 120 us (level)
  Pallas kernels: 63.9 us -> 65.2 us
    pallas_call x2, Pallas kernels: 61.3 us -> 62.6 us  [local_forces(): pl.pallas_call(functools.partial(force_kernel, side), out_shape=jax.Shape...]
where the time goes in v1:
time: 120 us; the launch traced here: 119 us
  Pallas kernels  65.2 us (54%)
  starting transfers between devices  22.4 us (19%)
  waiting for transfers between devices  12.7 us (11%)
  between operations  10.2 us (8%)
  other arithmetic  5.09 us (4%)
  local copies, waits for them, and re-layouts  3.15 us (3%)
    pallas_call x2, Pallas kernels, local_forces(): pl.pallas_call(functools.partial(force_kernel, side), out_shape=jax.Shape...  62.6 us
    ppermute x15, starting transfers between devices, from_behind(): return lax.ppermute(block, axis, route)  22.4 us
    ppermute x15, waiting for transfers between devices, from_behind(): return lax.ppermute(block, axis, route)  12.7 us
    unnamed x17, local copies, waits for them, and re-layouts  2.92 us
    pallas_call x1, Pallas kernels, bond_matrices(): pl.pallas_call(functools.partial(bond_kernel, side), out_shape=jax.ShapeD...  2.6 us
  transfers between devices with their start and end apart: 15, of which 8 were waited for; matrix products, arithmetic and copies ran while one was open for 2% of the time, Pallas kernels for 2%

profile of v1, /device:TPU:1, one launch (start us, length us, event | category | flops | bytes accessed | tf_op | source)
XLA Modules:
  0.0 118.7 jit_solution(8103471154027787244)
XLA Ops:
  0.6 0.8 fusion.9
  1.4 0.8 broadcast_select_fusion.1
  2.3 2.2 %collective-permute-start = (f32[3,1,3,3,128]{4,3,2,1,0:T(4,128)S(1)}, f32[3,1,3,3,128]{4,3,2,1,0:T(4,128)S(1)}, u32[]{:S(2)}, u32[]{:S(2)}) collective-permute-start(f32[3,1,3,3,128]{4,3,2,1,0:T(4,128)S(1)} %get-tuple-element.29), channel_id=1, source_target_pairs={{24,0},{0,8},{8,16},{16,24},{25,1},{1,9},{9,17},{17,25},{26,2},{2,... | collective-permute-start | bytes 41480 | tf_op jit(solution)/shard_map/ppermute | solution.py:23
  4.4 2.1 %collective-permute-start.1 = (f32[3,1,3,3,128]{4,3,2,1,0:T(4,128)S(1)}, f32[3,1,3,3,128]{4,3,2,1,0:T(4,128)S(1)}, u32[]{:S(2)}, u32[]{:S(2)}) collective-permute-start(f32[3,1,3,3,128]{4,3,2,1,0:T(4,128)S(1)} %get-tuple-element.30), channel_id=1, source_target_pairs={{8,0},{16,8},{24,16},{0,24},{9,1},{17,9},{25,17},{1,25},{10,2},{18... | collective-permute-start | bytes 41480 | tf_op jit(solution)/shard_map/ppermute | solution.py:23
  6.5 0.7 copy-done.4
  7.2 0.1 select_reduce_fusion
  7.3 0.3 collective-permute-done
  7.6 1.3 %collective-permute-start.2 = (f32[3,5,1,3,128]{4,3,2,1,0:T(4,128)S(1)}, f32[3,5,1,3,128]{4,3,2,1,0:T(4,128)S(1)}, u32[]{:S(2)}, u32[]{:S(2)}) collective-permute-start(f32[3,5,1,3,128]{4,3,2,1,0:T(4,128)S(1)} %get-tuple-element.25), channel_id=1, source_target_pairs={{4,0},{0,4},{5,1},{1,5},{6,2},{2,6},{7,3},{3,7},{12,8},{8,12},{13,... | collective-permute-start | bytes 69128 | tf_op jit(solution)/shard_map/ppermute | solution.py:23
  8.9 0.2 collective-permute-start.3
  9.2 0.1 select_reduce_fusion.1
  9.3 1.2 %collective-permute-done.2 = f32[3,5,1,3,128]{4,3,2,1,0:T(4,128)S(1)} collective-permute-done((f32[3,5,1,3,128]{4,3,2,1,0:T(4,128)S(1)}, f32[3,5,1,3,128]{4,3,2,1,0:T(4,128)S(1)}, u32[]{:S(2)}, u32[]{:S(2)}) %collective-permute-start.2) | collective-permute-done | bytes 23072 | tf_op jit(solution)/shard_map/ppermute | solution.py:23
  10.4 1.2 %collective-permute-done.3 = f32[3,5,1,3,128]{4,3,2,1,0:T(4,128)S(1)} collective-permute-done((f32[3,5,1,3,128]{4,3,2,1,0:T(4,128)S(1)}, f32[3,5,1,3,128]{4,3,2,1,0:T(4,128)S(1)}, u32[]{:S(2)}, u32[]{:S(2)}) %collective-permute-start.3) | collective-permute-done | bytes 23072 | tf_op jit(solution)/shard_map/ppermute | solution.py:23
  11.7 0.1 pad_maximum_fusion.12
  11.8 0.0 copy-start.6
  11.8 4.3 %collective-permute-start.4 = (f32[3,5,5,1,128]{4,3,2,1,0:T(1,128)S(1)}, f32[3,5,5,1,128]{4,3,2,1,0:T(1,128)S(1)}, u32[]{:S(2)}, u32[]{:S(2)}) collective-permute-start(f32[3,5,5,1,128]{4,3,2,1,0:T(1,128)S(1)} %get-tuple-element.21), channel_id=1, source_target_pairs={{3,0},{0,1},{1,2},{2,3},{7,4},{4,5},{5,6},{6,7},{11,8},{8,9},{9,10... | collective-permute-start | bytes 115208 | tf_op jit(solution)/shard_map/ppermute | solution.py:23
  16.1 0.7 fusion.13
  16.9 0.7 copy-done
  17.5 2.6 %bond_matrices.1.lap_ref = bf16[9,3,128,128]{3,2,1,0:T(8,128)(2,1)S(1)} custom-call(s32[3,3,3]{2,1,0:T(4,128)S(1)} %copy-done, s32[2,3,3,3,128]{4,3,2,1,0:T(4,128)S(1)} %copy.13.bonds_ref), custom_call_target="tpu_custom_call" | custom-call | flops 113246208 | bytes 884736 | tf_op jit(solution)/shard_map/bond_matrices/pallas_call | solution.py:128
  20.2 0.1 pad_maximum_fusion.ext_ref
  20.3 0.0 copy-start.1
  20.3 0.0 copy-start.2
  20.3 31.6 %cell_forces.2 = f32[3,3,3,3,128]{4,3,2,1,0:T(4,128)} custom-call(s32[3,3,3]{2,1,0:T(4,128)S(1)} %copy-done, f32[3,5,5,5,128]{4,3,2,1,0:T(8,128)S(1)} %pad_maximum_fusion.ext_ref, bf16[9,3,128,128]{3,2,1,0:T(8,128)(2,1)S(1)} %bond_matrices.1.lap_ref), custom_call_target="tpu_custom_call" | custom-call | tf_op jit(solution)/shard_map/cell_forces/pallas_call | solution.py:149
  51.9 0.9 broadcast_select_fusion
  52.8 0.9 collective-permute-start.6
  53.7 2.4 %collective-permute-start.7 = (f32[3,1,3,3,128]{4,3,2,1,0:T(4,128)S(1)}, f32[3,1,3,3,128]{4,3,2,1,0:T(4,128)S(1)}, u32[]{:S(2)}, u32[]{:S(2)}) collective-permute-start(f32[3,1,3,3,128]{4,3,2,1,0:T(4,128)S(1)} %get-tuple-element.28), channel_id=1, source_target_pairs={{8,0},{16,8},{24,16},{0,24},{9,1},{17,9},{25,17},{1,25},{10,2},{18... | collective-permute-start | bytes 41480 | tf_op jit(solution)/shard_map/ppermute | solution.py:23
  56.1 0.1 select_reduce_fusion.2
  56.3 1.0 collective-permute-done.6
  57.3 1.1 collective-permute-start.8
  58.4 0.5 collective-permute-start.9
  58.8 0.7 select_reduce_fusion.3
  65.1 0.1 pad_maximum_fusion.7
  65.1 3.0 %collective-permute-start.10 = (f32[3,5,5,1,128]{4,3,2,1,0:T(1,128)S(1)}, f32[3,5,5,1,128]{4,3,2,1,0:T(1,128)S(1)}, u32[]{:S(2)}, u32[]{:S(2)}) collective-permute-start(f32[3,5,5,1,128]{4,3,2,1,0:T(1,128)S(1)} %get-tuple-element.19), channel_id=1, source_target_pairs={{3,0},{0,1},{1,2},{2,3},{7,4},{4,5},{5,6},{6,7},{11,8},{8,9},{9,10... | collective-permute-start | bytes 115208 | tf_op jit(solution)/shard_map/ppermute | solution.py:23
  68.1 0.1 pad_dynamic-slice_fusion.5
  69.5 2.0 %collective-permute-done.11 = f32[3,5,5,1,128]{4,3,2,1,0:T(1,128)S(1)} collective-permute-done((f32[3,5,5,1,128]{4,3,2,1,0:T(1,128)S(1)}, f32[3,5,5,1,128]{4,3,2,1,0:T(1,128)S(1)}, u32[]{:S(2)}, u32[]{:S(2)}) %collective-permute-start.11) | collective-permute-done | bytes 38432 | tf_op jit(solution)/shard_map/ppermute | solution.py:23
  71.5 0.1 pad_maximum_fusion.1.ext_ref
  71.6 31.0 %cell_forces.3 = f32[3,3,3,3,128]{4,3,2,1,0:T(4,128)S(1)} custom-call(s32[3,3,3]{2,1,0:T(4,128)S(1)} %copy-done, f32[3,5,5,5,128]{4,3,2,1,0:T(8,128)S(1)} %pad_maximum_fusion.1.ext_ref, bf16[9,3,128,128]{3,2,1,0:T(8,128)(2,1)S(1)} %bond_matrices.1.lap_ref), custom_call_target="tpu_custom_call" | custom-call | tf_op jit(solution)/shard_map/cell_forces/pallas_call | solution.py:149
  102.7 2.6 %collective-permute-start.12 = (f32[6,2,3,3,128]{4,3,2,1,0:T(4,128)S(1)}, f32[6,2,3,3,128]{4,3,2,1,0:T(4,128)S(1)}, u32[]{:S(2)}, u32[]{:S(2)}) collective-permute-start(f32[6,2,3,3,128]{4,3,2,1,0:T(4,128)S(1)} %pad_maximum_fusion.2), channel_id=1, source_target_pairs={{8,0},{16,8},{24,16},{0,24},{9,1},{17,9},{25,17},{1,25},{10,2},{18... | collective-permute-start | bytes 165896 | tf_op jit(solution)/shard_map/ppermute | solution.py:23
  106.5 0.3 collective-permute-done.12
  106.7 0.1 fusion.8
  106.9 1.0 collective-permute-start.13
  107.9 4.0 %collective-permute-done.13 = f32[6,5,2,3,128]{4,3,2,1,0:T(4,128)S(1)} collective-permute-done((f32[6,5,2,3,128]{4,3,2,1,0:T(4,128)S(1)}, f32[6,5,2,3,128]{4,3,2,1,0:T(4,128)S(1)}, u32[]{:S(2)}, u32[]{:S(2)}) %collective-permute-start.13) | collective-permute-done | bytes 92192 | tf_op jit(solution)/shard_map/ppermute | solution.py:23
  111.9 0.1 fusion.4
  112.1 0.1 slice.73
  112.1 0.8 collective-permute-start.14
  114.3 2.6 %collective-permute-done.14 = f32[6,5,5,2,128]{4,3,2,1,0:T(2,128)S(1)} collective-permute-done((f32[6,5,5,2,128]{4,3,2,1,0:T(2,128)S(1)}, f32[6,5,5,2,128]{4,3,2,1,0:T(2,128)S(1)}, u32[]{:S(2)}, u32[]{:S(2)}) %collective-permute-start.14) | collective-permute-done | bytes 153632 | tf_op jit(solution)/shard_map/ppermute | solution.py:23
  116.8 0.3 fusion.1
  117.2 0.8 copy.14
  117.9 0.8 copy.15
  (32 shorter events, 0.2 us)
Async XLA Ops:
  2.3 5.4 %collective-permute-start = (f32[3,1,3,3,128]{4,3,2,1,0:T(4,128)S(1)}, f32[3,1,3,3,128]{4,3,2,1,0:T(4,128)S(1)}, u32[]{:S(2)}, u32[]{:S(2)}) collective-permute-start(f32[3,1,3,3,128]{4,3,2,1,0:T(4,128)S(1)} %get-tuple-element.29), channel_id=1, source_target_pairs={{24,0},{0,8},{8,16},{16,24},{25,1},{1,9},{9,17},{17,25},{26,2},{2,... | collective-permute-start | bytes 41480 | tf_op jit(solution)/shard_map/ppermute | solution.py:23
  4.4 3.2 %collective-permute-start.1 = (f32[3,1,3,3,128]{4,3,2,1,0:T(4,128)S(1)}, f32[3,1,3,3,128]{4,3,2,1,0:T(4,128)S(1)}, u32[]{:S(2)}, u32[]{:S(2)}) collective-permute-start(f32[3,1,3,3,128]{4,3,2,1,0:T(4,128)S(1)} %get-tuple-element.30), channel_id=1, source_target_pairs={{8,0},{16,8},{24,16},{0,24},{9,1},{17,9},{25,17},{1,25},{10,2},{18... | collective-permute-start | bytes 41480 | tf_op jit(solution)/shard_map/ppermute | solution.py:23
  6.5 0.7 copy-start.4
  7.6 2.8 %collective-permute-start.2 = (f32[3,5,1,3,128]{4,3,2,1,0:T(4,128)S(1)}, f32[3,5,1,3,128]{4,3,2,1,0:T(4,128)S(1)}, u32[]{:S(2)}, u32[]{:S(2)}) collective-permute-start(f32[3,5,1,3,128]{4,3,2,1,0:T(4,128)S(1)} %get-tuple-element.25), channel_id=1, source_target_pairs={{4,0},{0,4},{5,1},{1,5},{6,2},{2,6},{7,3},{3,7},{12,8},{8,12},{13,... | collective-permute-start | bytes 69128 | tf_op jit(solution)/shard_map/ppermute | solution.py:23
  8.9 2.7 %collective-permute-start.3 = (f32[3,5,1,3,128]{4,3,2,1,0:T(4,128)S(1)}, f32[3,5,1,3,128]{4,3,2,1,0:T(4,128)S(1)}, u32[]{:S(2)}, u32[]{:S(2)}) collective-permute-start(f32[3,5,1,3,128]{4,3,2,1,0:T(4,128)S(1)} %get-tuple-element.26), channel_id=1, source_target_pairs={{4,0},{0,4},{5,1},{1,5},{6,2},{2,6},{7,3},{3,7},{12,8},{8,12},{13,... | collective-permute-start | bytes 69128 | tf_op jit(solution)/shard_map/ppermute | solution.py:23
  11.7 5.2 %copy-start.3 = (s32[2,3,3,3,128]{4,0,3,2,1:T(2,128)S(1)}, s32[2,3,3,3,128]{4,0,3,2,1:T(2,128)}, u32[]{:S(2)}) copy-start(s32[2,3,3,3,128]{4,0,3,2,1:T(2,128)} %param.10) | copy-start | bytes 82948
  11.8 4.4 %copy-start.6 = (s32[4]{0:T(128)S(1)}, s32[4]{0:T(128)}, u32[]{:S(2)}) copy-start(s32[4]{0:T(128)} %param.11) | copy-start | bytes 52
  11.8 8.4 %collective-permute-start.4 = (f32[3,5,5,1,128]{4,3,2,1,0:T(1,128)S(1)}, f32[3,5,5,1,128]{4,3,2,1,0:T(1,128)S(1)}, u32[]{:S(2)}, u32[]{:S(2)}) collective-permute-start(f32[3,5,5,1,128]{4,3,2,1,0:T(1,128)S(1)} %get-tuple-element.21), channel_id=1, source_target_pairs={{3,0},{0,1},{1,2},{2,3},{7,4},{4,5},{5,6},{6,7},{11,8},{8,9},{9,10... | collective-permute-start | bytes 115208 | tf_op jit(solution)/shard_map/ppermute | solution.py:23
  16.1 4.1 %collective-permute-start.5 = (f32[3,5,5,1,128]{4,3,2,1,0:T(1,128)S(1)}, f32[3,5,5,1,128]{4,3,2,1,0:T(1,128)S(1)}, u32[]{:S(2)}, u32[]{:S(2)}) collective-permute-start(f32[3,5,5,1,128]{4,3,2,1,0:T(1,128)S(1)} %get-tuple-element.22), channel_id=1, source_target_pairs={{1,0},{2,1},{3,2},{0,3},{5,4},{6,5},{7,6},{4,7},{9,8},{10,9},{11,1... | collective-permute-start | bytes 115208 | tf_op jit(solution)/shard_map/ppermute | solution.py:23
  16.9 0.7 copy-start
  20.3 31.6 %copy-start.1 = (f32[3,3,3,3,128]{4,3,2,1,0:T(4,128)S(1)}, f32[3,3,3,3,128]{4,3,2,1,0:T(4,128)}, u32[]{:S(2)}) copy-start(f32[3,3,3,3,128]{4,3,2,1,0:T(4,128)} %param.7) | copy-start | bytes 124420
  20.3 31.6 %copy-start.2 = (f32[3,3,3,3,128]{4,3,2,1,0:T(4,128)S(1)}, f32[3,3,3,3,128]{4,3,2,1,0:T(4,128)}, u32[]{:S(2)}) copy-start(f32[3,3,3,3,128]{4,3,2,1,0:T(4,128)} %param.8) | copy-start | bytes 124420
  52.8 3.3 %copy-start.5 = (s32[4,2]{0,1:T(2,128)S(1)}, s32[4,2]{0,1:T(2,128)}, u32[]{:S(2)}) copy-start(s32[4,2]{0,1:T(2,128)} %param.12) | copy-start | bytes 100
  52.8 4.5 %collective-permute-start.6 = (f32[3,1,3,3,128]{4,3,2,1,0:T(4,128)S(1)}, f32[3,1,3,3,128]{4,3,2,1,0:T(4,128)S(1)}, u32[]{:S(2)}, u32[]{:S(2)}) collective-permute-start(f32[3,1,3,3,128]{4,3,2,1,0:T(4,128)S(1)} %get-tuple-element.27), channel_id=1, source_target_pairs={{24,0},{0,8},{8,16},{16,24},{25,1},{1,9},{9,17},{17,25},{26,2},{2,... | collective-permute-start | bytes 41480 | tf_op jit(solution)/shard_map/ppermute | solution.py:23
  53.7 3.6 %collective-permute-start.7 = (f32[3,1,3,3,128]{4,3,2,1,0:T(4,128)S(1)}, f32[3,1,3,3,128]{4,3,2,1,0:T(4,128)S(1)}, u32[]{:S(2)}, u32[]{:S(2)}) collective-permute-start(f32[3,1,3,3,128]{4,3,2,1,0:T(4,128)S(1)} %get-tuple-element.28), channel_id=1, source_target_pairs={{8,0},{16,8},{24,16},{0,24},{9,1},{17,9},{25,17},{1,25},{10,2},{18... | collective-permute-start | bytes 41480 | tf_op jit(solution)/shard_map/ppermute | solution.py:23
  57.3 7.7 %collective-permute-start.8 = (f32[3,5,1,3,128]{4,3,2,1,0:T(4,128)S(1)}, f32[3,5,1,3,128]{4,3,2,1,0:T(4,128)S(1)}, u32[]{:S(2)}, u32[]{:S(2)}) collective-permute-start(f32[3,5,1,3,128]{4,3,2,1,0:T(4,128)S(1)} %get-tuple-element.23), channel_id=1, source_target_pairs={{4,0},{0,4},{5,1},{1,5},{6,2},{2,6},{7,3},{3,7},{12,8},{8,12},{13,... | collective-permute-start | bytes 69128 | tf_op jit(solution)/shard_map/ppermute | solution.py:23
  58.4 6.7 %collective-permute-start.9 = (f32[3,5,1,3,128]{4,3,2,1,0:T(4,128)S(1)}, f32[3,5,1,3,128]{4,3,2,1,0:T(4,128)S(1)}, u32[]{:S(2)}, u32[]{:S(2)}) collective-permute-start(f32[3,5,1,3,128]{4,3,2,1,0:T(4,128)S(1)} %get-tuple-element.24), channel_id=1, source_target_pairs={{4,0},{0,4},{5,1},{1,5},{6,2},{2,6},{7,3},{3,7},{12,8},{8,12},{13,... | collective-permute-start | bytes 69128 | tf_op jit(solution)/shard_map/ppermute | solution.py:23
  65.1 4.3 %collective-permute-start.10 = (f32[3,5,5,1,128]{4,3,2,1,0:T(1,128)S(1)}, f32[3,5,5,1,128]{4,3,2,1,0:T(1,128)S(1)}, u32[]{:S(2)}, u32[]{:S(2)}) collective-permute-start(f32[3,5,5,1,128]{4,3,2,1,0:T(1,128)S(1)} %get-tuple-element.19), channel_id=1, source_target_pairs={{3,0},{0,1},{1,2},{2,3},{7,4},{4,5},{5,6},{6,7},{11,8},{8,9},{9,10... | collective-permute-start | bytes 115208 | tf_op jit(solution)/shard_map/ppermute | solution.py:23
  68.1 3.4 %collective-permute-start.11 = (f32[3,5,5,1,128]{4,3,2,1,0:T(1,128)S(1)}, f32[3,5,5,1,128]{4,3,2,1,0:T(1,128)S(1)}, u32[]{:S(2)}, u32[]{:S(2)}) collective-permute-start(f32[3,5,5,1,128]{4,3,2,1,0:T(1,128)S(1)} %get-tuple-element.20), channel_id=1, source_target_pairs={{1,0},{2,1},{3,2},{0,3},{5,4},{6,5},{7,6},{4,7},{9,8},{10,9},{11,1... | collective-permute-start | bytes 115208 | tf_op jit(solution)/shard_map/ppermute | solution.py:23
  102.7 4.1 %collective-permute-start.12 = (f32[6,2,3,3,128]{4,3,2,1,0:T(4,128)S(1)}, f32[6,2,3,3,128]{4,3,2,1,0:T(4,128)S(1)}, u32[]{:S(2)}, u32[]{:S(2)}) collective-permute-start(f32[6,2,3,3,128]{4,3,2,1,0:T(4,128)S(1)} %pad_maximum_fusion.2), channel_id=1, source_target_pairs={{8,0},{16,8},{24,16},{0,24},{9,1},{17,9},{25,17},{1,25},{10,2},{18... | collective-permute-start | bytes 165896 | tf_op jit(solution)/shard_map/ppermute | solution.py:23
  106.9 5.1 %collective-permute-start.13 = (f32[6,5,2,3,128]{4,3,2,1,0:T(4,128)S(1)}, f32[6,5,2,3,128]{4,3,2,1,0:T(4,128)S(1)}, u32[]{:S(2)}, u32[]{:S(2)}) collective-permute-start(f32[6,5,2,3,128]{4,3,2,1,0:T(4,128)S(1)} %slice.72), channel_id=1, source_target_pairs={{4,0},{0,4},{5,1},{1,5},{6,2},{2,6},{7,3},{3,7},{12,8},{8,12},{13,... | collective-permute-start | bytes 276488 | tf_op jit(solution)/shard_map/ppermute | solution.py:23
  112.1 4.7 %collective-permute-start.14 = (f32[6,5,5,2,128]{4,3,2,1,0:T(2,128)S(1)}, f32[6,5,5,2,128]{4,3,2,1,0:T(2,128)S(1)}, u32[]{:S(2)}, u32[]{:S(2)}) collective-permute-start(f32[6,5,5,2,128]{4,3,2,1,0:T(2,128)S(1)} %slice.73), channel_id=1, source_target_pairs={{1,0},{2,1},{3,2},{0,3},{5,4},{6,5},{7,6},{4,7},{9,8},{10,9},{11,1... | collective-permute-start | bytes 460808 | tf_op jit(solution)/shard_map/ppermute | solution.py:23

commit v2 on v1

--- a/solution.py
+++ b/solution.py
@@ -13,8 +13,8 @@
 BOND_STIFF = 1.0
 STEP_DT = 0.2
 FAR_AWAY = 1000.0
-UNIT = math.sqrt(1.0 / (SPREAD * math.log(2.0)))
-ROWS = 32
+UNIT = math.sqrt(1.0 / SPREAD)
+ROWS = 8
 
 
 def from_behind(block, axis, distance):
@@ -92,7 +92,7 @@
                             distance = (
                                 apart[0] * apart[0] + apart[1] * apart[1] + apart[2] * apart[2]
                             )
-                            weight = jnp.exp2(-distance)
+                            weight = jnp.exp(-distance)
                             total = [total[k] + weight * apart[k] for k in range(3)]
                 for k in range(3):
                     sum_ref[k * side + x, rows, :] = total[k]

time: 120 us -> 126 us (1.050); the launches traced: 119 us -> 126 us
  Pallas kernels: 65.2 us -> 70.3 us
  starting transfers between devices: 22.4 us -> 24.1 us
    pallas_call x2, Pallas kernels: 62.6 us -> 67.7 us  [local_forces(): pl.pallas_call(functools.partial(force_kernel, side), out_shape=jax.Shape...]
    ppermute x15, starting transfers between devices: 22.4 us -> 24.1 us  [from_behind(): return lax.ppermute(block, axis, route)]
  transfers between devices with their start and end apart: 15 -> 15, of which waited for: 8 -> 8; matrix products, arithmetic and copies ran while one was open for 2% -> 1% of each run, Pallas kernels for 2% -> 2%
where the time goes in v2:
time: 126 us
  Pallas kernels  70.3 us (56%)
  starting transfers between devices  24.1 us (19%)
  waiting for transfers between devices  13.5 us (11%)
  between operations  10.2 us (8%)
  other arithmetic  5.09 us (4%)
  local copies, waits for them, and re-layouts  3.15 us (2%)
    pallas_call x2, Pallas kernels, local_forces(): pl.pallas_call(functools.partial(force_kernel, side), out_shape=jax.Shape...  67.7 us
    ppermute x15, starting transfers between devices, from_behind(): return lax.ppermute(block, axis, route)  24.1 us
    ppermute x15, waiting for transfers between devices, from_behind(): return lax.ppermute(block, axis, route)  13.5 us
    unnamed x17, local copies, waits for them, and re-layouts  2.92 us
    pallas_call x1, Pallas kernels, bond_matrices(): pl.pallas_call(functools.partial(bond_kernel, side), out_shape=jax.ShapeD...  2.6 us
  transfers between devices with their start and end apart: 15, of which 8 were waited for; matrix products, arithmetic and copies ran while one was open for 1% of the time, Pallas kernels for 2%

profile of v2, /device:TPU:1, one launch (start us, length us, event | category | flops | bytes accessed | tf_op | source)
XLA Modules:
  0.0 126.3 jit_solution(2533372978395810985)
XLA Ops:
  0.6 0.8 fusion.9
  1.4 0.8 broadcast_select_fusion.1
  2.3 2.2 %collective-permute-start = (f32[3,1,3,3,128]{4,3,2,1,0:T(4,128)S(1)}, f32[3,1,3,3,128]{4,3,2,1,0:T(4,128)S(1)}, u32[]{:S(2)}, u32[]{:S(2)}) collective-permute-start(f32[3,1,3,3,128]{4,3,2,1,0:T(4,128)S(1)} %get-tuple-element.29), channel_id=1, source_target_pairs={{24,0},{0,8},{8,16},{16,24},{25,1},{1,9},{9,17},{17,25},{26,2},{2,... | collective-permute-start | bytes 41480 | tf_op jit(solution)/shard_map/ppermute | solution.py:23
  4.4 2.1 %collective-permute-start.1 = (f32[3,1,3,3,128]{4,3,2,1,0:T(4,128)S(1)}, f32[3,1,3,3,128]{4,3,2,1,0:T(4,128)S(1)}, u32[]{:S(2)}, u32[]{:S(2)}) collective-permute-start(f32[3,1,3,3,128]{4,3,2,1,0:T(4,128)S(1)} %get-tuple-element.30), channel_id=1, source_target_pairs={{8,0},{16,8},{24,16},{0,24},{9,1},{17,9},{25,17},{1,25},{10,2},{18... | collective-permute-start | bytes 41480 | tf_op jit(solution)/shard_map/ppermute | solution.py:23
  6.5 0.7 copy-done.4
  7.2 0.1 select_reduce_fusion
  7.3 0.3 collective-permute-done
  7.6 1.3 %collective-permute-start.2 = (f32[3,5,1,3,128]{4,3,2,1,0:T(4,128)S(1)}, f32[3,5,1,3,128]{4,3,2,1,0:T(4,128)S(1)}, u32[]{:S(2)}, u32[]{:S(2)}) collective-permute-start(f32[3,5,1,3,128]{4,3,2,1,0:T(4,128)S(1)} %get-tuple-element.25), channel_id=1, source_target_pairs={{4,0},{0,4},{5,1},{1,5},{6,2},{2,6},{7,3},{3,7},{12,8},{8,12},{13,... | collective-permute-start | bytes 69128 | tf_op jit(solution)/shard_map/ppermute | solution.py:23
  8.9 0.2 collective-permute-start.3
  9.2 0.1 select_reduce_fusion.1
  9.3 1.2 collective-permute-done.2
  10.4 1.2 collective-permute-done.3
  11.7 0.1 pad_maximum_fusion.12
  11.8 0.0 copy-start.6
  11.8 4.3 %collective-permute-start.4 = (f32[3,5,5,1,128]{4,3,2,1,0:T(1,128)S(1)}, f32[3,5,5,1,128]{4,3,2,1,0:T(1,128)S(1)}, u32[]{:S(2)}, u32[]{:S(2)}) collective-permute-start(f32[3,5,5,1,128]{4,3,2,1,0:T(1,128)S(1)} %get-tuple-element.21), channel_id=1, source_target_pairs={{3,0},{0,1},{1,2},{2,3},{7,4},{4,5},{5,6},{6,7},{11,8},{8,9},{9,10... | collective-permute-start | bytes 115208 | tf_op jit(solution)/shard_map/ppermute | solution.py:23
  16.1 0.7 fusion.13
  16.9 0.7 copy-done
  17.5 2.6 %bond_matrices.1.lap_ref = bf16[9,3,128,128]{3,2,1,0:T(8,128)(2,1)S(1)} custom-call(s32[3,3,3]{2,1,0:T(4,128)S(1)} %copy-done, s32[2,3,3,3,128]{4,3,2,1,0:T(4,128)S(1)} %copy.13.bonds_ref), custom_call_target="tpu_custom_call" | custom-call | flops 113246208 | bytes 884736 | tf_op jit(solution)/shard_map/bond_matrices/pallas_call | solution.py:128
  20.2 0.1 pad_maximum_fusion.ext_ref
  20.3 0.0 copy-start.1
  20.3 0.0 copy-start.2
  20.3 34.2 %cell_forces.2 = f32[3,3,3,3,128]{4,3,2,1,0:T(4,128)} custom-call(s32[3,3,3]{2,1,0:T(4,128)S(1)} %copy-done, f32[3,5,5,5,128]{4,3,2,1,0:T(8,128)S(1)} %pad_maximum_fusion.ext_ref, bf16[9,3,128,128]{3,2,1,0:T(8,128)(2,1)S(1)} %bond_matrices.1.lap_ref), custom_call_target="tpu_custom_call" | custom-call | tf_op jit(solution)/shard_map/cell_forces/pallas_call | solution.py:149
  54.5 0.9 broadcast_select_fusion
  55.4 1.0 collective-permute-start.6
  56.3 4.4 %collective-permute-start.7 = (f32[3,1,3,3,128]{4,3,2,1,0:T(4,128)S(1)}, f32[3,1,3,3,128]{4,3,2,1,0:T(4,128)S(1)}, u32[]{:S(2)}, u32[]{:S(2)}) collective-permute-start(f32[3,1,3,3,128]{4,3,2,1,0:T(4,128)S(1)} %get-tuple-element.28), channel_id=1, source_target_pairs={{8,0},{16,8},{24,16},{0,24},{9,1},{17,9},{25,17},{1,25},{10,2},{18... | collective-permute-start | bytes 41480 | tf_op jit(solution)/shard_map/ppermute | solution.py:23
  60.7 0.1 select_reduce_fusion.2
  60.8 1.0 collective-permute-done.6
  61.8 0.1 collective-permute-start.8
  61.9 1.5 %collective-permute-start.9 = (f32[3,5,1,3,128]{4,3,2,1,0:T(4,128)S(1)}, f32[3,5,1,3,128]{4,3,2,1,0:T(4,128)S(1)}, u32[]{:S(2)}, u32[]{:S(2)}) collective-permute-start(f32[3,5,1,3,128]{4,3,2,1,0:T(4,128)S(1)} %get-tuple-element.24), channel_id=1, source_target_pairs={{4,0},{0,4},{5,1},{1,5},{6,2},{2,6},{7,3},{3,7},{12,8},{8,12},{13,... | collective-permute-start | bytes 69128 | tf_op jit(solution)/shard_map/ppermute | solution.py:23
  63.4 0.7 select_reduce_fusion.3
  69.6 0.1 pad_maximum_fusion.7
  69.6 1.7 %collective-permute-start.10 = (f32[3,5,5,1,128]{4,3,2,1,0:T(1,128)S(1)}, f32[3,5,5,1,128]{4,3,2,1,0:T(1,128)S(1)}, u32[]{:S(2)}, u32[]{:S(2)}) collective-permute-start(f32[3,5,5,1,128]{4,3,2,1,0:T(1,128)S(1)} %get-tuple-element.19), channel_id=1, source_target_pairs={{3,0},{0,1},{1,2},{2,3},{7,4},{4,5},{5,6},{6,7},{11,8},{8,9},{9,10... | collective-permute-start | bytes 115208 | tf_op jit(solution)/shard_map/ppermute | solution.py:23
  71.4 0.1 pad_dynamic-slice_fusion.5
  72.7 2.0 %collective-permute-done.11 = f32[3,5,5,1,128]{4,3,2,1,0:T(1,128)S(1)} collective-permute-done((f32[3,5,5,1,128]{4,3,2,1,0:T(1,128)S(1)}, f32[3,5,5,1,128]{4,3,2,1,0:T(1,128)S(1)}, u32[]{:S(2)}, u32[]{:S(2)}) %collective-permute-start.11) | collective-permute-done | bytes 38432 | tf_op jit(solution)/shard_map/ppermute | solution.py:23
  74.8 0.1 pad_maximum_fusion.1.ext_ref
  74.9 33.5 %cell_forces.3 = f32[3,3,3,3,128]{4,3,2,1,0:T(4,128)S(1)} custom-call(s32[3,3,3]{2,1,0:T(4,128)S(1)} %copy-done, f32[3,5,5,5,128]{4,3,2,1,0:T(8,128)S(1)} %pad_maximum_fusion.1.ext_ref, bf16[9,3,128,128]{3,2,1,0:T(8,128)(2,1)S(1)} %bond_matrices.1.lap_ref), custom_call_target="tpu_custom_call" | custom-call | tf_op jit(solution)/shard_map/cell_forces/pallas_call | solution.py:149
  108.4 5.0 %collective-permute-start.12 = (f32[6,2,3,3,128]{4,3,2,1,0:T(4,128)S(1)}, f32[6,2,3,3,128]{4,3,2,1,0:T(4,128)S(1)}, u32[]{:S(2)}, u32[]{:S(2)}) collective-permute-start(f32[6,2,3,3,128]{4,3,2,1,0:T(4,128)S(1)} %pad_maximum_fusion.2), channel_id=1, source_target_pairs={{8,0},{16,8},{24,16},{0,24},{9,1},{17,9},{25,17},{1,25},{10,2},{18... | collective-permute-start | bytes 165896 | tf_op jit(solution)/shard_map/ppermute | solution.py:23
  114.6 0.1 collective-permute-done.12
  114.8 0.1 fusion.8
  114.9 0.1 collective-permute-start.13
  115.0 4.5 %collective-permute-done.13 = f32[6,5,2,3,128]{4,3,2,1,0:T(4,128)S(1)} collective-permute-done((f32[6,5,2,3,128]{4,3,2,1,0:T(4,128)S(1)}, f32[6,5,2,3,128]{4,3,2,1,0:T(4,128)S(1)}, u32[]{:S(2)}, u32[]{:S(2)}) %collective-permute-start.13) | collective-permute-done | bytes 92192 | tf_op jit(solution)/shard_map/ppermute | solution.py:23
  119.5 0.1 fusion.4
  119.7 0.1 slice.73
  119.7 0.3 collective-permute-start.14
  121.4 3.1 %collective-permute-done.14 = f32[6,5,5,2,128]{4,3,2,1,0:T(2,128)S(1)} collective-permute-done((f32[6,5,5,2,128]{4,3,2,1,0:T(2,128)S(1)}, f32[6,5,5,2,128]{4,3,2,1,0:T(2,128)S(1)}, u32[]{:S(2)}, u32[]{:S(2)}) %collective-permute-start.14) | collective-permute-done | bytes 153632 | tf_op jit(solution)/shard_map/ppermute | solution.py:23
  124.4 0.3 fusion.1
  124.8 0.8 copy.14
  125.5 0.8 copy.15
  (32 shorter events, 0.2 us)
Async XLA Ops:
  2.3 5.4 %collective-permute-start = (f32[3,1,3,3,128]{4,3,2,1,0:T(4,128)S(1)}, f32[3,1,3,3,128]{4,3,2,1,0:T(4,128)S(1)}, u32[]{:S(2)}, u32[]{:S(2)}) collective-permute-start(f32[3,1,3,3,128]{4,3,2,1,0:T(4,128)S(1)} %get-tuple-element.29), channel_id=1, source_target_pairs={{24,0},{0,8},{8,16},{16,24},{25,1},{1,9},{9,17},{17,25},{26,2},{2,... | collective-permute-start | bytes 41480 | tf_op jit(solution)/shard_map/ppermute | solution.py:23
  4.4 3.2 %collective-permute-start.1 = (f32[3,1,3,3,128]{4,3,2,1,0:T(4,128)S(1)}, f32[3,1,3,3,128]{4,3,2,1,0:T(4,128)S(1)}, u32[]{:S(2)}, u32[]{:S(2)}) collective-permute-start(f32[3,1,3,3,128]{4,3,2,1,0:T(4,128)S(1)} %get-tuple-element.30), channel_id=1, source_target_pairs={{8,0},{16,8},{24,16},{0,24},{9,1},{17,9},{25,17},{1,25},{10,2},{18... | collective-permute-start | bytes 41480 | tf_op jit(solution)/shard_map/ppermute | solution.py:23
  6.5 0.7 copy-start.4
  7.6 2.8 %collective-permute-start.2 = (f32[3,5,1,3,128]{4,3,2,1,0:T(4,128)S(1)}, f32[3,5,1,3,128]{4,3,2,1,0:T(4,128)S(1)}, u32[]{:S(2)}, u32[]{:S(2)}) collective-permute-start(f32[3,5,1,3,128]{4,3,2,1,0:T(4,128)S(1)} %get-tuple-element.25), channel_id=1, source_target_pairs={{4,0},{0,4},{5,1},{1,5},{6,2},{2,6},{7,3},{3,7},{12,8},{8,12},{13,... | collective-permute-start | bytes 69128 | tf_op jit(solution)/shard_map/ppermute | solution.py:23
  8.9 2.7 %collective-permute-start.3 = (f32[3,5,1,3,128]{4,3,2,1,0:T(4,128)S(1)}, f32[3,5,1,3,128]{4,3,2,1,0:T(4,128)S(1)}, u32[]{:S(2)}, u32[]{:S(2)}) collective-permute-start(f32[3,5,1,3,128]{4,3,2,1,0:T(4,128)S(1)} %get-tuple-element.26), channel_id=1, source_target_pairs={{4,0},{0,4},{5,1},{1,5},{6,2},{2,6},{7,3},{3,7},{12,8},{8,12},{13,... | collective-permute-start | bytes 69128 | tf_op jit(solution)/shard_map/ppermute | solution.py:23
  11.7 5.2 %copy-start.3 = (s32[2,3,3,3,128]{4,0,3,2,1:T(2,128)S(1)}, s32[2,3,3,3,128]{4,0,3,2,1:T(2,128)}, u32[]{:S(2)}) copy-start(s32[2,3,3,3,128]{4,0,3,2,1:T(2,128)} %param.10) | copy-start | bytes 82948
  11.8 4.4 %copy-start.6 = (s32[4]{0:T(128)S(1)}, s32[4]{0:T(128)}, u32[]{:S(2)}) copy-start(s32[4]{0:T(128)} %param.11) | copy-start | bytes 52
  11.8 8.4 %collective-permute-start.4 = (f32[3,5,5,1,128]{4,3,2,1,0:T(1,128)S(1)}, f32[3,5,5,1,128]{4,3,2,1,0:T(1,128)S(1)}, u32[]{:S(2)}, u32[]{:S(2)}) collective-permute-start(f32[3,5,5,1,128]{4,3,2,1,0:T(1,128)S(1)} %get-tuple-element.21), channel_id=1, source_target_pairs={{3,0},{0,1},{1,2},{2,3},{7,4},{4,5},{5,6},{6,7},{11,8},{8,9},{9,10... | collective-permute-start | bytes 115208 | tf_op jit(solution)/shard_map/ppermute | solution.py:23
  16.1 4.1 %collective-permute-start.5 = (f32[3,5,5,1,128]{4,3,2,1,0:T(1,128)S(1)}, f32[3,5,5,1,128]{4,3,2,1,0:T(1,128)S(1)}, u32[]{:S(2)}, u32[]{:S(2)}) collective-permute-start(f32[3,5,5,1,128]{4,3,2,1,0:T(1,128)S(1)} %get-tuple-element.22), channel_id=1, source_target_pairs={{1,0},{2,1},{3,2},{0,3},{5,4},{6,5},{7,6},{4,7},{9,8},{10,9},{11,1... | collective-permute-start | bytes 115208 | tf_op jit(solution)/shard_map/ppermute | solution.py:23
  16.9 0.7 copy-start
  20.3 34.2 %copy-start.1 = (f32[3,3,3,3,128]{4,3,2,1,0:T(4,128)S(1)}, f32[3,3,3,3,128]{4,3,2,1,0:T(4,128)}, u32[]{:S(2)}) copy-start(f32[3,3,3,3,128]{4,3,2,1,0:T(4,128)} %param.7) | copy-start | bytes 124420
  20.3 34.2 %copy-start.2 = (f32[3,3,3,3,128]{4,3,2,1,0:T(4,128)S(1)}, f32[3,3,3,3,128]{4,3,2,1,0:T(4,128)}, u32[]{:S(2)}) copy-start(f32[3,3,3,3,128]{4,3,2,1,0:T(4,128)} %param.8) | copy-start | bytes 124420
  55.4 5.4 %copy-start.5 = (s32[4,2]{0,1:T(2,128)S(1)}, s32[4,2]{0,1:T(2,128)}, u32[]{:S(2)}) copy-start(s32[4,2]{0,1:T(2,128)} %param.12) | copy-start | bytes 100
  55.4 6.4 %collective-permute-start.6 = (f32[3,1,3,3,128]{4,3,2,1,0:T(4,128)S(1)}, f32[3,1,3,3,128]{4,3,2,1,0:T(4,128)S(1)}, u32[]{:S(2)}, u32[]{:S(2)}) collective-permute-start(f32[3,1,3,3,128]{4,3,2,1,0:T(4,128)S(1)} %get-tuple-element.27), channel_id=1, source_target_pairs={{24,0},{0,8},{8,16},{16,24},{25,1},{1,9},{9,17},{17,25},{26,2},{2,... | collective-permute-start | bytes 41480 | tf_op jit(solution)/shard_map/ppermute | solution.py:23
  56.3 5.5 %collective-permute-start.7 = (f32[3,1,3,3,128]{4,3,2,1,0:T(4,128)S(1)}, f32[3,1,3,3,128]{4,3,2,1,0:T(4,128)S(1)}, u32[]{:S(2)}, u32[]{:S(2)}) collective-permute-start(f32[3,1,3,3,128]{4,3,2,1,0:T(4,128)S(1)} %get-tuple-element.28), channel_id=1, source_target_pairs={{8,0},{16,8},{24,16},{0,24},{9,1},{17,9},{25,17},{1,25},{10,2},{18... | collective-permute-start | bytes 41480 | tf_op jit(solution)/shard_map/ppermute | solution.py:23
  61.8 7.7 %collective-permute-start.8 = (f32[3,5,1,3,128]{4,3,2,1,0:T(4,128)S(1)}, f32[3,5,1,3,128]{4,3,2,1,0:T(4,128)S(1)}, u32[]{:S(2)}, u32[]{:S(2)}) collective-permute-start(f32[3,5,1,3,128]{4,3,2,1,0:T(4,128)S(1)} %get-tuple-element.23), channel_id=1, source_target_pairs={{4,0},{0,4},{5,1},{1,5},{6,2},{2,6},{7,3},{3,7},{12,8},{8,12},{13,... | collective-permute-start | bytes 69128 | tf_op jit(solution)/shard_map/ppermute | solution.py:23
  61.9 7.7 %collective-permute-start.9 = (f32[3,5,1,3,128]{4,3,2,1,0:T(4,128)S(1)}, f32[3,5,1,3,128]{4,3,2,1,0:T(4,128)S(1)}, u32[]{:S(2)}, u32[]{:S(2)}) collective-permute-start(f32[3,5,1,3,128]{4,3,2,1,0:T(4,128)S(1)} %get-tuple-element.24), channel_id=1, source_target_pairs={{4,0},{0,4},{5,1},{1,5},{6,2},{2,6},{7,3},{3,7},{12,8},{8,12},{13,... | collective-permute-start | bytes 69128 | tf_op jit(solution)/shard_map/ppermute | solution.py:23
  69.6 3.1 %collective-permute-start.10 = (f32[3,5,5,1,128]{4,3,2,1,0:T(1,128)S(1)}, f32[3,5,5,1,128]{4,3,2,1,0:T(1,128)S(1)}, u32[]{:S(2)}, u32[]{:S(2)}) collective-permute-start(f32[3,5,5,1,128]{4,3,2,1,0:T(1,128)S(1)} %get-tuple-element.19), channel_id=1, source_target_pairs={{3,0},{0,1},{1,2},{2,3},{7,4},{4,5},{5,6},{6,7},{11,8},{8,9},{9,10... | collective-permute-start | bytes 115208 | tf_op jit(solution)/shard_map/ppermute | solution.py:23
  71.4 3.4 %collective-permute-start.11 = (f32[3,5,5,1,128]{4,3,2,1,0:T(1,128)S(1)}, f32[3,5,5,1,128]{4,3,2,1,0:T(1,128)S(1)}, u32[]{:S(2)}, u32[]{:S(2)}) collective-permute-start(f32[3,5,5,1,128]{4,3,2,1,0:T(1,128)S(1)} %get-tuple-element.20), channel_id=1, source_target_pairs={{1,0},{2,1},{3,2},{0,3},{5,4},{6,5},{7,6},{4,7},{9,8},{10,9},{11,1... | collective-permute-start | bytes 115208 | tf_op jit(solution)/shard_map/ppermute | solution.py:23
  108.4 6.4 %collective-permute-start.12 = (f32[6,2,3,3,128]{4,3,2,1,0:T(4,128)S(1)}, f32[6,2,3,3,128]{4,3,2,1,0:T(4,128)S(1)}, u32[]{:S(2)}, u32[]{:S(2)}) collective-permute-start(f32[6,2,3,3,128]{4,3,2,1,0:T(4,128)S(1)} %pad_maximum_fusion.2), channel_id=1, source_target_pairs={{8,0},{16,8},{24,16},{0,24},{9,1},{17,9},{25,17},{1,25},{10,2},{18... | collective-permute-start | bytes 165896 | tf_op jit(solution)/shard_map/ppermute | solution.py:23
  114.9 4.6 %collective-permute-start.13 = (f32[6,5,2,3,128]{4,3,2,1,0:T(4,128)S(1)}, f32[6,5,2,3,128]{4,3,2,1,0:T(4,128)S(1)}, u32[]{:S(2)}, u32[]{:S(2)}) collective-permute-start(f32[6,5,2,3,128]{4,3,2,1,0:T(4,128)S(1)} %slice.72), channel_id=1, source_target_pairs={{4,0},{0,4},{5,1},{1,5},{6,2},{2,6},{7,3},{3,7},{12,8},{8,12},{13,... | collective-permute-start | bytes 276488 | tf_op jit(solution)/shard_map/ppermute | solution.py:23
  119.7 4.7 %collective-permute-start.14 = (f32[6,5,5,2,128]{4,3,2,1,0:T(2,128)S(1)}, f32[6,5,5,2,128]{4,3,2,1,0:T(2,128)S(1)}, u32[]{:S(2)}, u32[]{:S(2)}) collective-permute-start(f32[6,5,5,2,128]{4,3,2,1,0:T(2,128)S(1)} %slice.73), channel_id=1, source_target_pairs={{1,0},{2,1},{3,2},{0,3},{5,4},{6,5},{7,6},{4,7},{9,8},{10,9},{11,1... | collective-permute-start | bytes 460808 | tf_op jit(solution)/shard_map/ppermute | solution.py:23
